TPU v7x, 128 devices: a whole 4x4x4 slice. The times are simulated.
128 devices in a mesh: dp: 16 (over z, y_lo, core), head: 8 (over x, y_hi).
Axes of the slice: x: 4, y: 4 (y_hi: 2, y_lo: 2; y = y_hi * 2 + y_lo), z: 4, core: 2. Of those that a mesh axis runs over, the one named last changes fastest.
Arguments:
- resp_query: bfloat16 [16384, 8192], P(('dp', 'head')), may hold values from -6 to 6
- resp_keyval: bfloat16 [16384, 2048], P(('dp', 'head')), may hold values from -6 to 6
- grad_out: bfloat16 [16384, 8192], P(('dp', 'head')), may hold values from -6 to 6
- prompt_keyval: bfloat16 [8192, 2048], P('dp', 'head'), may hold values from -6 to 6
- response_prompt: int32 [32], P('dp'), may hold values from 0 to 7, as said below
- piece_owner: int32 [16], replicated, may hold values from 0 to 15, each once
Outputs:
- attn_out: bfloat16 [16384, 8192], P(('dp', 'head'))
- grad_query: bfloat16 [16384, 8192], P(('dp', 'head'))
- grad_keyval: bfloat16 [16384, 2048], P(('dp', 'head'))
- grad_prompt: bfloat16 [8192, 2048], P('dp', 'head')
Inputs may be any that keep to these rules, and one draw needn't show every extreme that they name: `response_prompt`: every prompt has 2 to 8 responses; one prompt has exactly 8 and one exactly 2. `piece_owner`: each slot holds exactly one half of one prompt.
All inputs are finite; a program needn't handle non-finite values.
Results may differ from a plain program's by a relative error of at most 0.023.
Values may be sent and summed in bfloat16 or wider, within the bound.
A program may use at most 192 MiB of HBM per device.

v0:
```python
import jax
import jax.numpy as jnp
from jax import lax
from jax.sharding import PartitionSpec as P

QH = 64
KVH = 8
DH = 128
RL = 512
PLH = 512
RESP_DEV = 2


NEGATIVE = -1e30


def online_update(stats, scores, allowed, value_rows, formula):
    maximum, normalizer, accumulated = stats
    visible = jnp.asarray(allowed).astype(jnp.float32)
    masked = jnp.where(allowed, scores, NEGATIVE)
    fresh = jnp.maximum(maximum, jnp.max(masked, axis=-1))
    weights = jnp.exp(masked - fresh[..., None]) * visible
    normalizer = jnp.sum(weights, axis=-1)
    product = jnp.einsum(
        formula, weights.astype(jnp.bfloat16), value_rows, preferred_element_type=jnp.float32
    )
    accumulated = product
    return (fresh, normalizer, accumulated)


def merge_stats(first_stats, second_stats):
    maximum = jnp.maximum(first_stats[0], second_stats[0])
    first_factor = jnp.exp(first_stats[0] - maximum)
    second_factor = jnp.exp(second_stats[0] - maximum)
    normalizer = first_stats[1] * first_factor + second_stats[1] * second_factor
    accumulated = (
        first_stats[2] * first_factor[..., None] + second_stats[2] * second_factor[..., None]
    )
    return (maximum, normalizer, accumulated)


def back_block(queries, cotangent, key_rows, value_rows, allowed, log_total, delta, score_scale):
    visible = jnp.asarray(allowed).astype(jnp.float32)
    scores = (
        jnp.einsum("rtkgd,rskd->rkgts", queries, key_rows, preferred_element_type=jnp.float32)
        * score_scale
    )
    probs = jnp.exp(jnp.where(allowed, scores, NEGATIVE) - log_total[..., None]) * visible
    dprobs = jnp.einsum(
        "rtkgd,rskd->rkgts", cotangent, value_rows, preferred_element_type=jnp.float32
    )
    dscores = (probs * (dprobs - delta[..., None]) * score_scale).astype(jnp.bfloat16)
    grad_q = jnp.einsum("rkgts,rskd->rtkgd", dscores, key_rows, preferred_element_type=jnp.float32)
    grad_k = jnp.einsum("rkgts,rtkgd->rskd", dscores, queries, preferred_element_type=jnp.float32)
    grad_v = jnp.einsum(
        "rkgts,rtkgd->rskd",
        probs.astype(jnp.bfloat16),
        cotangent,
        preferred_element_type=jnp.float32,
    )
    return (grad_q, grad_k, grad_v)


def lookup(table, positions, width):
    hits = positions[..., None] == jnp.arange(width, dtype=jnp.int32)
    return jnp.sum(jnp.where(hits, table, 0), axis=-1)


def body(resp_query, resp_keyval, grad_out, prompt_keyval, response_prompt, piece_owner):
    heads = lax.axis_size("head")
    devices = lax.axis_size("dp")
    local_kv = KVH // heads
    groups = QH // KVH
    tok_here = resp_query.shape[0]
    columns = prompt_keyval.shape[1]
    score_scale = DH ** (-0.5)
    query3 = resp_query.reshape(tok_here, KVH, groups * DH)
    pair3 = resp_keyval.reshape(tok_here, KVH, 2 * DH)
    cot3 = grad_out.reshape(tok_here, KVH, groups * DH)
    query_all, pair_all, cot_all = (
        lax.all_to_all(query3, "head", split_axis=1, concat_axis=0, tiled=True),
        lax.all_to_all(pair3, "head", split_axis=1, concat_axis=0, tiled=True),
        lax.all_to_all(cot3, "head", split_axis=1, concat_axis=0, tiled=True),
    )
    queries = query_all.reshape(RESP_DEV, RL, local_kv, groups, DH)
    cotangent = cot_all.reshape(RESP_DEV, RL, local_kv, groups, DH)
    pairs = pair_all.reshape(RESP_DEV, RL, local_kv, 2, DH)
    own_keys = pairs[:, :, :, 0]
    own_values = pairs[:, :, :, 1]
    wanted = 2 * response_prompt[:, None] + jnp.arange(2, dtype=jnp.int32)[None, :]
    needed = lookup(piece_owner, wanted, devices)
    empty_stats = (
        jnp.full((RESP_DEV, local_kv, groups, RL), NEGATIVE, jnp.float32),
        jnp.zeros((RESP_DEV, local_kv, groups, RL), jnp.float32),
        jnp.zeros((RESP_DEV, local_kv, groups, RL, DH), jnp.float32),
    )
    causal = jnp.arange(RL)[:, None] >= jnp.arange(RL)[None, :]
    self_scores = (
        jnp.einsum("rtkgd,rukd->rkgtu", queries, own_keys, preferred_element_type=jnp.float32)
        * score_scale
    )
    self_stats = online_update(empty_stats, self_scores, causal, own_values, "rkgtu,rukd->rkgtd")
    kept_start = jnp.zeros((RESP_DEV, 2, PLH, columns), jnp.bfloat16)
    offsets = jnp.arange(PLH, dtype=jnp.int32)
    kept = kept_start
    piece = lax.all_gather(prompt_keyval, "dp", axis=0, tiled=True)
    rows = piece.shape[0]
    for keep_response in range(RESP_DEV):
        for keep_half_index in range(2):
            places = needed[keep_response, keep_half_index] * PLH + offsets
            inside = (places >= 0) & (places < rows)
            taken = jnp.take(piece, jnp.clip(places, 0, rows - 1), axis=0)
            update = jnp.where(inside[:, None], taken, kept[keep_response, keep_half_index])
            kept = kept.at[keep_response, keep_half_index].set(update)
    whole = kept.reshape(RESP_DEV, 2 * PLH, local_kv, 2, DH)
    scores = (
        jnp.einsum(
            "rtkgd,rskd->rkgts", queries, whole[:, :, :, 0], preferred_element_type=jnp.float32
        )
        * score_scale
    )
    prefix_stats = online_update(
        empty_stats, scores, jnp.array(True), whole[:, :, :, 1], "rkgts,rskd->rkgtd"
    )
    maximum, normalizer, accumulated = merge_stats(prefix_stats, self_stats)
    output_bf = (accumulated / normalizer[..., None]).astype(jnp.bfloat16)
    log_total = maximum + jnp.log(normalizer)
    output_tok = output_bf.transpose(0, 3, 1, 2, 4).reshape(RESP_DEV * RL, local_kv, groups * DH)
    output_back = lax.all_to_all(output_tok, "head", split_axis=0, concat_axis=1, tiled=True)
    attn_out = output_back.reshape(tok_here, QH * DH)
    delta = jnp.einsum(
        "rtkgd,rkgtd->rkgt", cotangent, output_bf, preferred_element_type=jnp.float32
    )
    grad_q, grad_k, grad_v = back_block(
        queries, cotangent, own_keys, own_values, causal, log_total, delta, score_scale
    )
    send_rows = jnp.zeros((devices, PLH, local_kv, 2, DH), jnp.float32)
    for half_index in range(2):
        part = kept[:, half_index].reshape(RESP_DEV, PLH, local_kv, 2, DH)
        prefix_q, prefix_k, prefix_v = back_block(
            queries,
            cotangent,
            part[:, :, :, 0],
            part[:, :, :, 1],
            jnp.array(True),
            log_total,
            delta,
            score_scale,
        )
        grad_q = grad_q + prefix_q
        stacked = jnp.stack([prefix_k, prefix_v], axis=3)
        for response in range(RESP_DEV):
            send_rows = send_rows.at[needed[response, half_index]].add(stacked[response])
    prompt_sum = lax.psum_scatter(
        send_rows.reshape(devices, PLH, columns).astype(jnp.bfloat16),
        "dp",
        scatter_dimension=0,
        tiled=True,
    ).astype(jnp.float32)
    grad_prompt = prompt_sum.reshape(PLH, columns).astype(jnp.bfloat16)
    query_grad3 = grad_q.astype(jnp.bfloat16).reshape(RESP_DEV * RL, local_kv, groups * DH)
    pair_grad3 = (
        jnp.stack([grad_k, grad_v], axis=3)
        .astype(jnp.bfloat16)
        .reshape(RESP_DEV * RL, local_kv, 2 * DH)
    )
    query_back, pair_back = (
        lax.all_to_all(query_grad3, "head", split_axis=0, concat_axis=1, tiled=True),
        lax.all_to_all(pair_grad3, "head", split_axis=0, concat_axis=1, tiled=True),
    )
    grad_query = query_back.reshape(tok_here, QH * DH)
    grad_keyval = pair_back.reshape(tok_here, KVH * 2 * DH)
    return (attn_out, grad_query, grad_keyval, grad_prompt)


def solution(mesh):
    placed = (
        P(("dp", "head"), None),
        P(("dp", "head"), None),
        P(("dp", "head"), None),
        P("dp", "head"),
        P("dp"),
        P(),
    )
    return jax.shard_map(
        body,
        mesh=mesh,
        in_specs=placed,
        out_specs=(
            P(("dp", "head"), None),
            P(("dp", "head"), None),
            P(("dp", "head"), None),
            P("dp", "head"),
        ),
        check_vma=False,
    )
```

profile of v0, /device:TPU:1, one launch (start us, length us, event | category | flops | bytes accessed | tf_op | source)
XLA Modules:
  0.0 480.6 jit_solution(2733578698470593507)
XLA Ops:
  9.8 7.5 %all-to-all-start.1 = ((bf16[128,8,256]{2,0,1:T(8,128)(2,1)}), bf16[128,8,256]{2,0,1:T(8,128)(2,1)S(1)}, u32[]{:S(2)}, u32[]{:S(2)}) async-start(bf16[128,8,256]{2,0,1:T(8,128)(2,1)} %bitcast.442), calls=%async_computation.1 | async-start | bytes 1048576 | tf_op jit(solution)/shard_map/all_to_all | solution.py:82
  20.4 7.1 %all-to-all-done.1 = bf16[128,8,256]{2,0,1:T(8,128)(2,1)S(1)} async-done(((bf16[128,8,256]{2,0,1:T(8,128)(2,1)}), bf16[128,8,256]{2,0,1:T(8,128)(2,1)S(1)}, u32[]{:S(2)}, u32[]{:S(2)}) %all-to-all-start.1) | async-done | bytes 524320 | tf_op jit(solution)/shard_map/all_to_all | solution.py:82
  27.5 4.6 all-to-all-start
  35.5 28.5 %all-to-all-done = bf16[128,8,1024]{2,0,1:T(8,128)(2,1)S(1)} async-done(((bf16[128,8,1024]{2,0,1:T(8,128)(2,1)}), bf16[128,8,1024]{2,0,1:T(8,128)(2,1)S(1)}, u32[]{:S(2)}, u32[]{:S(2)}) %all-to-all-start) | async-done | bytes 2097184 | tf_op jit(solution)/shard_map/all_to_all | solution.py:81
  64.1 4.4 all-to-all-start.3
  90.5 7.7 %all-to-all-done.3 = bf16[128,8,1024]{2,0,1:T(8,128)(2,1)} async-done(((bf16[128,8,1024]{2,0,1:T(8,128)(2,1)}), bf16[128,8,1024]{2,0,1:T(8,128)(2,1)}, u32[]{:S(2)}, u32[]{:S(2)}) %all-to-all-start.3) | async-done | bytes 2097184 | tf_op jit(solution)/shard_map/all_to_all | solution.py:83
  98.2 3.5 copy.279
  101.8 4.3 copy.217
  106.1 7.2 %fusion.24 = (f32[2,8,512]{2,1,0:T(8,128)S(1)}, f32[2,512,512,8]{2,1,3,0:T(8,128)}) fusion(pred[512,512]{0,1:T(8,128)(4,1)S(1)} %get-tuple-element.155, bf16[2,512,8,128]{1,3,2,0:T(8,128)(2,1)S(1)} %copy.215, bf16[2,512,1,1,128]{4,3,1,0,2:T(2,128)(2,1)S(1)} %copy-done.9), kind=kOutput, calls=%fused_computation.37 | convolution fusion | flops 1086316544 | bytes 19431424 | tf_op jit(solution)/shard_map/rtkgd,rukd->rkgtu/dot_general | solution.py:99
  113.4 13.7 %fusion.36 = f32[2,8,512,128]{3,2,1,0:T(8,128)} fusion(f32[2,512,512,8]{2,1,3,0:T(8,128)} %get-tuple-element.138, f32[512,512]{0,1:T(8,128)} %get-tuple-element.156, f32[2,8,512]{2,1,0:T(8,128)S(1)} %broadcast_maximum_fusion, pred[512,512]{0,1:T(8,128)(4,1)S(1)} %get-tuple-element.155, bf16[2,512,1,1,128]{4,3,1,0,2:T(2,128)(2,1)} %get-tuple-element.129), kind=kOutput, calls=%fused_computation.47 | convolution fusion | flops 1094713344 | bytes 22577152 | tf_op jit(solution)/shard_map/rkgtu,rukd->rkgtd/dot_general | solution.py:24
  127.0 8.0 %fusion.19 = f32[2,8,512]{2,1,0:T(8,128)S(1)} fusion(f32[2,512,512,8]{2,1,3,0:T(8,128)} %get-tuple-element.138, f32[512,512]{0,1:T(8,128)} %get-tuple-element.156, f32[2,8,512]{2,1,0:T(8,128)S(1)} %broadcast_maximum_fusion, pred[512,512]{0,1:T(8,128)(4,1)S(1)} %get-tuple-element.155), kind=kLoop, calls=%fused_computation.32 | loop fusion | flops 20963328 | bytes 18153472 | tf_op jit(solution)/shard_map/reduce_sum | solution.py:23
  135.1 4.3 gather_fusion
  140.6 4.8 %gather_fusion.1 = bf16[512,256]{1,0:T(8,128)(2,1)S(1)} fusion(bf16[8192,256]{1,0:T(8,128)(2,1)} %all-gather.2.cloned.1.call-done, s32[1024]{0:T(1024)S(1)} %pad_clamp_fusion.2), kind=kCustom, calls=%fused_computation.1.clone | custom fusion | bytes 526336 | tf_op jit(solution)/shard_map/jit(_take)/gather | solution.py:112
  147.6 4.3 gather_fusion.2
  153.8 4.3 gather_fusion.3
  164.2 3.3 fusion.107
  167.5 13.1 %bitcast_reduce_fusion = (f32[2,8,512]{2,1,0:T(8,128)S(1)}, f32[2,1024,512,8]{2,1,3,0:T(8,128)}) fusion(bf16[2,512,8,128]{1,3,2,0:T(8,128)(2,1)S(1)} %copy.215, bf16[2,1024,1,1,128]{4,3,1,0,2:T(2,128)(2,1)S(1)} %get-tuple-element.128), kind=kOutput, calls=%fused_computation.5 | convolution fusion | flops 2164252672 | bytes 36208640 | tf_op jit(solution)/shard_map/rtkgd,rskd->rkgts/dot_general | solution.py:117
  180.6 13.7 %fusion.1 = f32[2,8,512]{2,1,0:T(8,128)S(1)} fusion(f32[2,1024,512,8]{2,1,3,0:T(8,128)} %get-tuple-element.140, f32[2,8,512]{2,1,0:T(8,128)S(1)} %broadcast_maximum_fusion.1), kind=kLoop, calls=%fused_computation.7 | loop fusion | flops 25157632 | bytes 33619968 | tf_op jit(solution)/shard_map/reduce_sum | solution.py:23
  194.4 16.0 %fusion.111 = (f32[2,8,512,128]{3,2,1,0:T(8,128)S(1)}, bf16[2,8,512,128]{3,2,1,0:T(8,128)(2,1)}) fusion(f32[2,8,512]{2,1,0:T(8,128)S(1)} %get-tuple-element.122, f32[2,8,512,128]{3,2,1,0:T(8,128)S(1)} %copy-done.20, f32[2,8,512]{2,1,0:T(8,128)S(1)} %get-tuple-element.124, f32[2,8,512]{2,1,0:T(8,128)S(1)} %get-tuple-element.123, ...), kind=kOutput, calls=%fused_computation.170 | convolution fusion | flops 2178940928 | bytes 44695552 | tf_op jit(solution)/shard_map/rkgts,rskd->rkgtd/dot_general | solution.py:24
  213.3 8.1 %fusion.80 = f32[2,512,512,8]{2,1,3,0:T(8,128)} fusion(bf16[2,512,8,128]{1,3,2,0:T(8,128)(2,1)S(1)} %copy.215, bf16[2,512,1,2,128]{1,4,3,0,2:T(8,128)(2,1)S(1)} %bitcast.460), kind=kOutput, calls=%fused_computation.110 | convolution fusion | flops 1073741824 | bytes 19136512 | tf_op jit(solution)/shard_map/rtkgd,rskd->rkgts/dot_general | solution.py:45
  221.4 8.0 %fusion.53 = f32[2,512,1,1,128]{1,4,0,3,2:T(8,128)S(1)} fusion(bf16[2,512,8,128]{1,3,2,0:T(8,128)(2,1)} %copy.217, f32[2,512,512,8]{2,1,3,0:T(8,128)} %fusion.80, f32[2,8,512]{2,1,0:T(8,128)S(1)} %get-tuple-element.121), kind=kOutput, calls=%fused_computation.64 | convolution fusion | flops 1086324736 | bytes 19431424 | tf_op jit(solution)/shard_map/rkgts,rtkgd->rskd/dot_general | solution.py:55
  229.5 11.1 %fusion.30 = bf16[2,8,512,512]{2,3,1,0:T(8,128)(2,1)} fusion(f32[2,512,512,8]{2,1,3,0:T(8,128)} %fusion.80, f32[2,8,512]{2,1,0:T(8,128)S(1)} %copy.238, f32[2,8,512]{2,1,0:T(8,128)S(1)} %get-tuple-element.121, bf16[2,512,8,128]{1,3,2,0:T(8,128)(2,1)} %copy.217, bf16[2,512,1,2,128]{1,4,3,0,2:T(8,128)(2,1)S(1)} %bitcast.461), kind=kOutput, calls=%fused_computation.43 | convolution fusion | flops 1098907648 | bytes 27590656 | tf_op jit(solution)/shard_map/rtkgd,rskd->rkgts/dot_general | solution.py:49
  242.6 3.3 fusion.82
  245.9 5.7 %copy-done = f32[2,512,512,8]{2,1,3,0:T(8,128)} copy-done((f32[2,512,512,8]{2,1,3,0:T(8,128)}, f32[2,512,512,8]{2,1,3,0:T(8,128)S(1)}, u32[]{:S(2)}) %copy-start) | copy-done | bytes 16777240
  251.7 8.6 %fusion.31 = bf16[2,8,512,512]{2,3,1,0:T(8,128)(2,1)} fusion(f32[2,512,512,8]{2,1,3,0:T(8,128)S(1)} %fusion.82, f32[2,8,512]{2,1,0:T(8,128)} %copy-done.15, f32[2,8,512]{2,1,0:T(8,128)} %copy-done.12, bf16[2,512,8,128]{1,3,2,0:T(8,128)(2,1)} %copy.217, bf16[2,512,1,2,128]{1,4,3,0,2:T(8,128)(2,1)} %bitcast.458), kind=kOutput, calls=%fused_computation.44 | convolution fusion | flops 1098907648 | bytes 27590656 | tf_op jit(solution)/shard_map/rtkgd,rskd->rkgts/dot_general | solution.py:49
  260.2 8.0 %fusion.50 = f32[2,512,1,1,128]{1,4,0,3,2:T(8,128)S(1)} fusion(bf16[2,512,8,128]{1,3,2,0:T(8,128)(2,1)} %copy.217, f32[2,512,512,8]{2,1,3,0:T(8,128)} %copy-done, f32[2,8,512]{2,1,0:T(8,128)} %copy-done.12), kind=kOutput, calls=%fused_computation.63 | convolution fusion | flops 1086324736 | bytes 19431424 | tf_op jit(solution)/shard_map/rkgts,rtkgd->rskd/dot_general | solution.py:55
  268.3 6.3 %convolution_bitcast_fusion.1 = f32[2,512,1,1,128]{1,4,0,3,2:T(8,128)S(1)} fusion(bf16[2,8,512,512]{2,3,1,0:T(8,128)(2,1)} %fusion.30, bf16[2,512,8,128]{1,3,2,0:T(8,128)(2,1)S(1)} %copy.215), kind=kOutput, calls=%fused_computation.61 | convolution fusion | flops 1073741824 | bytes 11010048 | tf_op jit(solution)/shard_map/rkgts,rtkgd->rskd/dot_general | solution.py:54
  284.3 11.5 %fusion.29 = bf16[2,8,512,512]{2,3,1,0:T(8,128)(2,1)S(1)} fusion(f32[2,512,512,8]{2,1,3,0:T(8,128)} %get-tuple-element.138, f32[2,8,512]{2,1,0:T(8,128)S(1)} %copy-done.16, f32[2,8,512]{2,1,0:T(8,128)S(1)} %copy-done.13, f32[512,512]{0,1:T(8,128)} %get-tuple-element.156, pred[512,512]{0,1:T(8,128)(4,1)S(1)} %copy-done.5, ...), kind=kOutput, calls=%fused_computation.42 | convolution fusion | flops 1107296256 | bytes 28901376 | tf_op jit(solution)/shard_map/rtkgd,rskd->rkgts/dot_general | solution.py:49
  301.4 10.9 %fusion.60 = bf16[2,512,1,1,128]{4,1,0,3,2:T(8,128)(2,1)S(1)} fusion(bf16[2,512,8,128]{1,3,2,0:T(8,128)(2,1)} %copy.217, f32[2,512,512,8]{2,1,3,0:T(8,128)} %get-tuple-element.138, f32[2,8,512]{2,1,0:T(8,128)S(1)} %copy-done.13, f32[512,512]{0,1:T(8,128)} %get-tuple-element.156, pred[512,512]{0,1:T(8,128)(4,1)S(1)} %copy-done.5), kind=kOutput, calls=%fused_computation.67 | convolution fusion | flops 1094844416 | bytes 20480000 | tf_op jit(solution)/shard_map/rkgts,rtkgd->rskd/dot_general | solution.py:55
  313.7 3.8 reduce.48
  318.5 4.3 all-to-all-start.5
  322.8 7.0 %fusion.81 = f32[2,128,8,512]{1,3,2,0:T(8,128)S(1)} fusion(bf16[2,8,512,512]{2,3,1,0:T(8,128)(2,1)} %fusion.30, bf16[2,512,1,2,128]{1,4,3,0,2:T(8,128)(2,1)S(1)} %bitcast.462), kind=kOutput, calls=%fused_computation.111 | convolution fusion | flops 1073741824 | bytes 12845056 | tf_op jit(solution)/shard_map/rkgts,rskd->rtkgd/dot_general | solution.py:53
  329.9 8.9 %fusion.83 = f32[2,8,512,128]{3,2,1,0:T(8,128)} fusion(bf16[2,8,512,512]{2,3,1,0:T(8,128)(2,1)} %copy-done.3, bf16[2,512,1,1,128]{4,3,1,0,2:T(2,128)(2,1)S(1)} %copy-done.10), kind=kOutput, calls=%fused_computation.113 | convolution fusion | flops 1073741824 | bytes 12845056 | tf_op jit(solution)/shard_map/rkgts,rskd->rtkgd/dot_general | solution.py:53
  338.8 5.8 %fusion.46 = bf16[2,512,1,8,128]{4,1,3,0,2:T(8,128)(2,1)S(1)} fusion(bf16[2,8,512,512]{2,3,1,0:T(8,128)(2,1)S(1)} %bitcast.445, f32[2,128,8,512]{1,3,2,0:T(8,128)S(1)} %fusion.81, f32[2,8,512,128]{3,2,1,0:T(8,128)} %fusion.83, bf16[2,512,1,2,128]{1,4,3,0,2:T(8,128)(2,1)S(1)} %bitcast.459), kind=kOutput, calls=%fused_computation.58 | convolution fusion | flops 1076887552 | bytes 19136512 | tf_op jit(solution)/shard_map/rkgts,rskd->rtkgd/dot_general | solution.py:53
  347.3 12.7 %reshape.789 = bf16[1024,1,1024]{2,1,0:T(2,128)(2,1)} reshape(bf16[2,512,1,8,128]{4,3,1,0,2:T(8,128)(2,1)} %copy.206) | data formatting | bytes 4194304 | tf_op jit(solution)/shard_map/reshape | solution.py:161
  360.0 12.8 %reduce.47 = bf16[1024,1024]{1,0:T(8,128)(2,1)S(1)} reduce(bf16[1024,1,1024]{2,1,0:T(2,128)(2,1)} %reshape.789, bf16[]{:T(256)} %broadcast.398), dimensions={1}, to_apply=%reshape.789.reduce_sub_computation | reduce | bytes 4194306 | tf_op jit(solution)/shard_map/reshape | solution.py:161
  372.8 3.8 reshape.792
  376.6 6.6 %all-to-all-start.4 = ((bf16[8,2,65536]{2,1,0:T(2,128)(2,1)}), bf16[8,2,65536]{2,1,0:T(2,128)(2,1)S(1)}, u32[]{:S(2)}, u32[]{:S(2)}) async-start(bf16[8,2,65536]{2,1,0:T(2,128)(2,1)} %reshape.792), calls=%async_computation.4 | async-start | bytes 4194304 | tf_op jit(solution)/shard_map/all_to_all | solution.py:168
  383.3 4.3 copy.184
  387.5 12.5 %reshape.788 = bf16[1024,1,1024]{2,1,0:T(2,128)(2,1)} reshape(bf16[2,512,1,8,128]{4,3,1,0,2:T(8,128)(2,1)} %copy.184) | data formatting | bytes 4194304 | tf_op jit(solution)/shard_map/reshape | solution.py:128
  400.0 14.1 %reduce.46 = bf16[1024,1024]{1,0:T(8,128)(2,1)} reduce(bf16[1024,1,1024]{2,1,0:T(2,128)(2,1)} %reshape.788, bf16[]{:T(256)} %broadcast.398), dimensions={1}, to_apply=%reshape.788.reduce_sub_computation | reduce | bytes 4194306 | tf_op jit(solution)/shard_map/reshape | solution.py:128
  414.1 6.3 %reshape.790 = bf16[8,2,65536]{2,1,0:T(2,128)(2,1)} reshape(bf16[1024,1024]{1,0:T(8,128)(2,1)} %reduce.46) | data formatting | bytes 4194304
  420.4 6.6 %all-to-all-start.2 = ((bf16[8,2,65536]{2,1,0:T(2,128)(2,1)}), bf16[8,2,65536]{2,1,0:T(2,128)(2,1)}, u32[]{:S(2)}, u32[]{:S(2)}) async-start(bf16[8,2,65536]{2,1,0:T(2,128)(2,1)} %reshape.790), calls=%async_computation.2 | async-start | bytes 4194304 | tf_op jit(solution)/shard_map/all_to_all | solution.py:129
  432.5 4.4 reshape.793
  442.3 4.1 copy.224
  446.4 9.1 %all-to-all-done.2 = bf16[8,2,65536]{2,1,0:T(2,128)(2,1)} async-done(((bf16[8,2,65536]{2,1,0:T(2,128)(2,1)}), bf16[8,2,65536]{2,1,0:T(2,128)(2,1)}, u32[]{:S(2)}, u32[]{:S(2)}) %all-to-all-start.2) | async-done | bytes 2097184 | tf_op jit(solution)/shard_map/all_to_all | solution.py:129
  455.5 6.8 %reshape.791 = bf16[1024,1,1024]{2,1,0:T(2,128)(2,1)} reshape(bf16[8,2,65536]{2,1,0:T(2,128)(2,1)} %all-to-all-done.2) | data formatting | bytes 4194304
  467.7 4.1 copy.223
  (121 shorter events, 75.6 us)
Async XLA Ops:
  7.2 28.1 %copy-start.19 = (s32[2]{0:T(128)S(1)}, s32[2]{0:T(128)}, u32[]{:S(2)}) copy-start(s32[2]{0:T(128)} %param.28) | copy-start | bytes 28
  7.2 28.1 %copy-start.17 = (s32[16]{0:T(128)S(1)}, s32[16]{0:T(128)}, u32[]{:S(2)}) copy-start(s32[16]{0:T(128)} %param.29) | copy-start | bytes 196
  7.2 127.9 %all-gather.2.cloned.1.call-start = ((), (), s32[]{:S(2)}) async-start(), calls=%async_computation.7 | async-start | bytes 4456448 | tf_op jit(solution)/shard_map/all_gather | solution.py:106
  9.8 17.7 %all-to-all-start.1 = ((bf16[128,8,256]{2,0,1:T(8,128)(2,1)}), bf16[128,8,256]{2,0,1:T(8,128)(2,1)S(1)}, u32[]{:S(2)}, u32[]{:S(2)}) async-start(bf16[128,8,256]{2,0,1:T(8,128)(2,1)} %bitcast.442), calls=%async_computation.1 | async-start | bytes 1048576 | tf_op jit(solution)/shard_map/all_to_all | solution.py:82
  17.3 63.2 %copy-start.18 = (s32[5]{0:T(128)S(1)}, s32[5]{0:T(128)}, u32[]{:S(2)}) copy-start(s32[5]{0:T(128)} %constant.234.clone.1) | copy-start | bytes 64
  27.5 54.8 %copy-start.11 = (bf16[128,8,256]{2,0,1:T(8,128)(2,1)}, bf16[128,8,256]{2,0,1:T(8,128)(2,1)S(1)}, u32[]{:S(2)}) copy-start(bf16[128,8,256]{2,0,1:T(8,128)(2,1)S(1)} %all-to-all-done.1) | copy-start | bytes 1572868
  27.5 36.6 %all-to-all-start = ((bf16[128,8,1024]{2,0,1:T(8,128)(2,1)}), bf16[128,8,1024]{2,0,1:T(8,128)(2,1)S(1)}, u32[]{:S(2)}, u32[]{:S(2)}) async-start(bf16[128,8,1024]{2,0,1:T(8,128)(2,1)} %bitcast.453), calls=%async_computation | async-start | bytes 4194304 | tf_op jit(solution)/shard_map/all_to_all | solution.py:81
  64.1 34.2 %all-to-all-start.3 = ((bf16[128,8,1024]{2,0,1:T(8,128)(2,1)}), bf16[128,8,1024]{2,0,1:T(8,128)(2,1)}, u32[]{:S(2)}, u32[]{:S(2)}) async-start(bf16[128,8,1024]{2,0,1:T(8,128)(2,1)} %bitcast.452), calls=%async_computation.3 | async-start | bytes 4194304 | tf_op jit(solution)/shard_map/all_to_all | solution.py:83
  68.4 403.4 %reduce-scatter.2.cloned.1.call-start = ((), (), s32[]{:S(2)}) async-start(), calls=%async_computation.8 | async-start | bytes 4456448 | tf_op jit(solution)/shard_map/reduce_scatter | solution.py:154
  82.3 44.7 %copy-start.4 = (pred[512,512]{0,1:T(8,128)(4,1)}, pred[512,512]{0,1:T(8,128)(4,1)S(1)}, u32[]{:S(2)}) copy-start(pred[512,512]{0,1:T(8,128)(4,1)S(1)} %get-tuple-element.155) | copy-start | bytes 786436
  87.2 18.9 %copy-start.9 = (bf16[2,512,1,1,128]{4,3,1,0,2:T(2,128)(2,1)S(1)}, bf16[2,512,1,1,128]{4,3,1,0,2:T(2,128)(2,1)}, u32[]{:S(2)}) copy-start(bf16[2,512,1,1,128]{4,3,1,0,2:T(2,128)(2,1)} %get-tuple-element.130) | copy-start | bytes 786436
  180.6 13.8 %copy-start.20 = (f32[2,8,512,128]{3,2,1,0:T(8,128)S(1)}, f32[2,8,512,128]{3,2,1,0:T(8,128)}, u32[]{:S(2)}) copy-start(f32[2,8,512,128]{3,2,1,0:T(8,128)} %fusion.36) | copy-start | bytes 12582916
  194.4 35.1 %copy-start.12 = (f32[2,8,512]{2,1,0:T(8,128)}, f32[2,8,512]{2,1,0:T(8,128)S(1)}, u32[]{:S(2)}) copy-start(f32[2,8,512]{2,1,0:T(8,128)S(1)} %get-tuple-element.121) | copy-start | bytes 98308
  194.4 16.0 %copy-start.2 = (bf16[128,8,8,128]{3,2,1,0:T(8,128)(2,1)S(1)}, bf16[128,8,8,128]{3,2,1,0:T(8,128)(2,1)}, u32[]{:S(2)}) copy-start(bf16[128,8,8,128]{3,2,1,0:T(8,128)(2,1)} %copy.279) | copy-start | bytes 6291460
  213.1 16.4 %copy-start.15 = (f32[2,8,512]{2,1,0:T(8,128)}, f32[2,8,512]{2,1,0:T(8,128)S(1)}, u32[]{:S(2)}) copy-start(f32[2,8,512]{2,1,0:T(8,128)S(1)} %copy.238) | copy-start | bytes 98308
  213.3 16.2 %copy-start.7 = (bf16[2,1,512,256]{2,3,0,1:T(8,128)(2,1)}, bf16[2,1,512,256]{2,3,0,1:T(8,128)(2,1)S(1)}, u32[]{:S(2)}) copy-start(bf16[2,1,512,256]{2,3,0,1:T(8,128)(2,1)S(1)} %copy.190) | copy-start | bytes 1572868
  245.9 5.7 %copy-start = (f32[2,512,512,8]{2,1,3,0:T(8,128)}, f32[2,512,512,8]{2,1,3,0:T(8,128)S(1)}, u32[]{:S(2)}) copy-start(f32[2,512,512,8]{2,1,3,0:T(8,128)S(1)} %fusion.82) | copy-start | bytes 50331652
  268.3 6.3 %copy-start.1 = (bf16[2,8,512,512]{2,3,1,0:T(8,128)(2,1)S(1)}, bf16[2,8,512,512]{2,3,1,0:T(8,128)(2,1)}, u32[]{:S(2)}) copy-start(bf16[2,8,512,512]{2,3,1,0:T(8,128)(2,1)} %fusion.31) | copy-start | bytes 25165828
  282.0 2.3 copy-start.5
  282.0 2.3 copy-start.13
  282.0 2.3 copy-start.14
  282.0 2.3 copy-start.16
  295.8 3.2 copy-start.3
  301.4 21.4 %copy-start.8 = (bf16[2,1,512,256]{2,3,0,1:T(8,128)(2,1)S(1)}, bf16[2,1,512,256]{2,3,0,1:T(8,128)(2,1)}, u32[]{:S(2)}) copy-start(bf16[2,1,512,256]{2,3,0,1:T(8,128)(2,1)} %copy-done.7) | copy-start | bytes 1572868
  313.2 16.7 %copy-start.10 = (bf16[2,512,1,1,128]{4,3,1,0,2:T(2,128)(2,1)S(1)}, bf16[2,512,1,1,128]{4,3,1,0,2:T(2,128)(2,1)}, u32[]{:S(2)}) copy-start(bf16[2,512,1,1,128]{4,3,1,0,2:T(2,128)(2,1)} %get-tuple-element.130) | copy-start | bytes 786436
  318.5 58.2 %all-to-all-start.5 = ((bf16[8,2,16384]{2,1,0:T(2,128)(2,1)}), bf16[8,2,16384]{2,1,0:T(2,128)(2,1)}, u32[]{:S(2)}, u32[]{:S(2)}) async-start(bf16[8,2,16384]{2,1,0:T(2,128)(2,1)} %reshape.794), calls=%async_computation.5 | async-start | bytes 1048576 | tf_op jit(solution)/shard_map/all_to_all | solution.py:169
  322.8 16.0 %slice-start = ((s8[8388608]{0:T(1024)(128)(4,1)}), s8[4194304]{0:T(1024)(128)(4,1)S(1)}, s32[]{:S(2)}) async-start(s8[8388608]{0:T(1024)(128)(4,1)} %bitcast.444), calls=%async_computation.9 | async-start | bytes 8388608
  329.9 8.9 %slice-start.1 = ((s8[8388608]{0:T(1024)(128)(4,1)}), s8[4194304]{0:T(1024)(128)(4,1)S(1)}, s32[]{:S(2)}) async-start(s8[8388608]{0:T(1024)(128)(4,1)} %bitcast.444), calls=%async_computation.10 | async-start | bytes 8388608
  329.9 8.9 %copy-start.6 = (bf16[2,1,512,256]{2,3,0,1:T(8,128)(2,1)S(1)}, bf16[2,1,512,256]{2,3,0,1:T(8,128)(2,1)}, u32[]{:S(2)}) copy-start(bf16[2,1,512,256]{2,3,0,1:T(8,128)(2,1)} %copy.198) | copy-start | bytes 1572868
  376.6 43.8 %all-to-all-start.4 = ((bf16[8,2,65536]{2,1,0:T(2,128)(2,1)}), bf16[8,2,65536]{2,1,0:T(2,128)(2,1)S(1)}, u32[]{:S(2)}, u32[]{:S(2)}) async-start(bf16[8,2,65536]{2,1,0:T(2,128)(2,1)} %reshape.792), calls=%async_computation.4 | async-start | bytes 4194304 | tf_op jit(solution)/shard_map/all_to_all | solution.py:168
  420.4 35.1 %all-to-all-start.2 = ((bf16[8,2,65536]{2,1,0:T(2,128)(2,1)}), bf16[8,2,65536]{2,1,0:T(2,128)(2,1)}, u32[]{:S(2)}, u32[]{:S(2)}) async-start(bf16[8,2,65536]{2,1,0:T(2,128)(2,1)} %reshape.790), calls=%async_computation.2 | async-start | bytes 4194304 | tf_op jit(solution)/shard_map/all_to_all | solution.py:129
Sparse Core Ops, SparseCore 0:
  9.7 61.1 all-gather.1
  284.4 72.4 reduce-scatter.1
where the time goes:
time: 488 us; the launch traced here: 481 us
  matrix products  153 us (31%)
  local copies, waits for them, and re-layouts  149 us (31%)
  other arithmetic  66.9 us (14%)
  waiting for transfers between devices  53.2 us (11%)
  starting transfers between devices  34.1 us (7%)
  between operations  25.1 us (5%)
    unnamed x61, local copies, waits for them, and re-layouts  56.7 us
    dot_general x3, matrix products, back_block(): jnp.einsum('rtkgd,rskd->rkgts', cotangent, value_rows, preferred_element_...  31.1 us
    dot_general x2, matrix products, online_update(): jnp.einsum(formula, weights.astype(jnp.bfloat16), value_rows, preferred_e...  29.6 us
    all_to_all x1, waiting for transfers between devices, body(): lax.all_to_all(query3, 'head', split_axis=1, concat_axis=0, tiled=True)  28.5 us
    dot_general x3, matrix products, back_block(): jnp.einsum('rkgts,rtkgd->rskd', probs.astype(jnp.bfloat16), cotangent, pr...  27 us
    dot_general x3, matrix products, back_block(): jnp.einsum('rkgts,rskd->rtkgd', dscores, key_rows, preferred_element_type...  21.7 us
    reduce_sum x2, other arithmetic, online_update(): normalizer = jnp.sum(weights, axis=-1)  21.7 us
    gather x4, local copies, waits for them, and re-layouts, body(): taken = jnp.take(piece, jnp.clip(places, 0, rows - 1), axis=0)  17.7 us
  transfers between devices with their start and end apart: 8, of which 4 were waited for; matrix products, arithmetic and copies ran while one was open for 45% of the time, Pallas kernels for 0%

commit v1 on v0

v1 whole, which is shorter than its diff:
```python
import functools
import math

import jax
import jax.numpy as jnp
from jax import lax
from jax.experimental import pallas as pl
from jax.experimental.pallas import tpu as pltpu
from jax.sharding import PartitionSpec as P

DH = 128
GROUPS = 8
BLK = 128
PLH = 512
PL = 2 * PLH
KEYS = PL + 4 * BLK
WIDE = 2 * DH
SPAN = GROUPS * DH

CH = 4
GH = GROUPS // CH
CW = GH * DH
NB = 2
ROWS = GH * NB * BLK
KC = 256

SCALE = DH ** (-0.5)
SCALE2 = SCALE * math.log2(math.e)
NEGATIVE = -1e30
MESH = pl.DeviceIdType.MESH
BF = jnp.bfloat16
F32 = jnp.float32


def dot(a, b, ca, cb):
    return lax.dot_general(a, b, (((ca,), (cb,)), ((), ())), preferred_element_type=F32)


def attend(first, q, do, k, v, kt, vt, s, e, d, dk, dv):
    edge = PL + BLK * first
    total = edge + BLK * NB
    spans = [(at, min(KC, total - at)) for at in range(0, total, KC)]
    top = None
    for at, n in spans:
        part = dot(k[at : at + n], q, 1, 1)
        if at + n > edge:
            key = lax.broadcasted_iota(jnp.int32, (n, BLK), 0) + (at - edge)
            tok = lax.broadcasted_iota(jnp.int32, (n, BLK), 1)
            seen = jnp.concatenate(
                [key <= tok + BLK * b for b in range(NB) for _ in range(GH)], axis=1
            )
            part = jnp.where(seen, part, NEGATIVE)
        s[at : at + n] = part
        high = jnp.max(part.reshape(n // 8, 8, ROWS), axis=0)
        top = high if top is None else jnp.maximum(top, high)
    peak = jnp.max(top, axis=0, keepdims=True) * SCALE2
    for at, n in spans:
        e[at : at + n] = jnp.exp2(s[at : at + n] * SCALE2 - peak).astype(BF)
    mixed = dot(vt[:, :total], e[:total], 1, 0)
    inverse = 1.0 / mixed[DH : DH + 1]
    out = (mixed[:DH] * inverse).astype(BF)
    cot = do.T.astype(F32)
    delta = jnp.sum(cot * out.astype(F32), axis=0, keepdims=True) * inverse
    scaled = (cot * inverse).astype(BF)
    for at, n in spans:
        dp = dot(v[at : at + n], scaled, 1, 0)
        d[at : at + n] = (e[at : at + n].astype(F32) * (dp - delta)).astype(BF)
    dq = (dot(kt[:, :total], d[:total], 1, 0) * SCALE).astype(BF)
    for at, n in spans:
        dk[at : at + n] += dot(d[at : at + n], q, 1, 0)
        dv[at : at + n] += dot(e[at : at + n], scaled, 1, 1)
    return out.T, dq.T


def kernel(
    q_hbm, do_hbm, kv_hbm, pk_hbm, rp, po,
    o_hbm, dq_hbm, dkv_hbm, gp_hbm,
    qbuf, dobuf, kvbuf, pbuf, kbuf, vbuf, ktbuf, vtbuf, sbuf, ebuf, dbuf, dkbuf, dvbuf,
    obuf, dqbuf, dkvbuf, asend, arecv, bsend, brecv, csend, crecv, gpbuf,
    q_s, q_r, do_s, do_r, kv_s, kv_r, p_s, p_r, o_s, o_r, dq_s, dq_r, dkv_s, dkv_r,
    a_s, a_r, b_s, b_r, c_s, c_r, g_s,
):
    dp = lax.axis_index("dp")
    me = lax.axis_index("head")
    x, yh = me // 2, lax.rem(me, 2)
    z, yl, core = dp // 4, lax.rem(dp // 2, 2), lax.rem(dp, 2)

    def slot_of(zz, yy, cc):
        return (lax.rem(zz + 4, 4) * 2 + yy) * 2 + cc

    other_core = (slot_of(z, yl, 1 - core), me)
    other_y = (slot_of(z, 1 - yl, core), me)
    up = (slot_of(z + 1, yl, core), me)
    down = (slot_of(z - 1, yl, core), me)
    far = (slot_of(z + 2, yl, core), me)
    steps = [(1, 1), (3, 1), (2, 0), (2, 1), (0, 1), (1, 0), (3, 0)]
    peers = [lax.rem(x + a, 4) * 2 + lax.rem(yh + b, 2) for a, b in steps]

    barrier = pltpu.get_barrier_semaphore()
    friends = [(dp, h) for h in peers] + [other_core, other_y, up, down, far]
    for friend in friends:
        pl.semaphore_signal(barrier, inc=1, device_id=friend, device_id_type=MESH)
    pl.semaphore_wait(barrier, len(friends))

    def send(src, dst, ssem, rsem, to):
        pltpu.make_async_remote_copy(
            src_ref=src, dst_ref=dst, send_sem=ssem, recv_sem=rsem, device_id=to, device_id_type=MESH
        ).start()

    def local(src, dst, sem):
        pltpu.make_async_copy(src, dst, sem).start()

    def drain(ref, sem):
        pltpu.make_async_copy(ref, ref, sem).wait()

    mine = slot_of(z, yl, core)
    for to in (other_y, up, down, other_core):
        send(pk_hbm, pbuf.at[mine], p_s, p_r.at[mine], to)
    local(pk_hbm, pbuf.at[mine], p_r.at[mine])

    def cols(h, width, offset=0):
        return pl.ds(pl.multiple_of(h * (width) + offset, DH), width)

    for h in peers:
        send(kv_hbm.at[:, cols(h, WIDE)], kvbuf.at[me], kv_s, kv_r, (dp, h))
    local(kv_hbm.at[:, cols(me, WIDE)], kvbuf.at[me], kv_r)

    def heads_of(h, c):
        return pl.ds(pl.multiple_of(h * SPAN + c * CW, DH), CW)

    def push(c, carry):
        for h in peers:
            send(q_hbm.at[:, heads_of(h, c)], qbuf.at[c, me], q_s, q_r.at[c], (dp, h))
            send(do_hbm.at[:, heads_of(h, c)], dobuf.at[c, me], do_s, do_r.at[c], (dp, h))
        local(q_hbm.at[:, heads_of(me, c)], qbuf.at[c, me], q_r.at[c])
        local(do_hbm.at[:, heads_of(me, c)], dobuf.at[c, me], do_r.at[c])
        return carry

    lax.fori_loop(0, CH, push, 0)

    def forward(slot, targets):
        drain(pbuf.at[slot], p_r.at[slot])
        for to in targets:
            send(pbuf.at[slot], pbuf.at[slot], p_s, p_r.at[slot], to)

    forward(slot_of(z, 1 - yl, core), (up, down, other_core))
    forward(slot_of(z + 1, 0, core), (down, other_core))
    forward(slot_of(z - 1, 1, core), (up, other_core))
    forward(slot_of(z + 1, 1, core), (other_core,))
    forward(slot_of(z - 1, 0, core), (other_core,))
    forward(slot_of(z + 2, 0, core), (other_core,))
    forward(slot_of(z + 2, 1, core), (other_core,))
    drain(pbuf.at[mine], p_r.at[mine])
    for zz in range(4):
        for yy in range(2):
            slot = slot_of(zz, yy, 1 - core)
            drain(pbuf.at[slot], p_r.at[slot])
    drain(kvbuf, kv_r)

    need = [[po[2 * rp[r] + half] for half in range(2)] for r in range(2)]
    for r in range(2):
        for half in range(2):
            rows = slice(half * PLH, (half + 1) * PLH)
            both = pbuf[need[r][half]]
            kbuf[r, rows] = both[:, :DH]
            vbuf[r, rows] = both[:, DH:]
            ktbuf[r, :, rows] = both[:, :DH].T
            vtbuf[r, :DH, rows] = both[:, DH:].T
        for b in range(4):
            rows = slice(PL + b * BLK, PL + (b + 1) * BLK)
            both = kvbuf[r * 4 + b]
            kbuf[r, rows] = both[:, :DH]
            vbuf[r, rows] = both[:, DH:]
            ktbuf[r, :, rows] = both[:, :DH].T
            vtbuf[r, :DH, rows] = both[:, DH:].T
        vtbuf[r, DH:] = jnp.ones((16, KEYS), BF)
    dkbuf[...] = jnp.zeros_like(dkbuf)
    dvbuf[...] = jnp.zeros_like(dvbuf)

    def give(buf, hbm, ssem, rsem, c, h):
        @pl.when(h != me)
        def _():
            send(buf.at[c, h], hbm.at[:, heads_of(me, c)], ssem, rsem, (dp, h))

        @pl.when(h == me)
        def _():
            local(buf.at[c, h], hbm.at[:, heads_of(me, c)], rsem)

    def work(i, carry):
        c, r = i // 2, lax.rem(i, 2)

        @pl.when(r == 0)
        def _():
            drain(qbuf.at[c], q_r.at[c])
            drain(dobuf.at[c], do_r.at[c])

        for first in range(0, 4, NB):
            tiles = [(r * 4 + first + b, j) for b in range(NB) for j in range(GH)]
            q = jnp.concatenate([qbuf[c, h, :, j * DH : (j + 1) * DH] for h, j in tiles], axis=0)
            do = jnp.concatenate([dobuf[c, h, :, j * DH : (j + 1) * DH] for h, j in tiles], axis=0)
            w = first // NB % 2
            out, dq = attend(
                first, q, do, kbuf.at[r], vbuf.at[r], ktbuf.at[r], vtbuf.at[r],
                sbuf.at[w], ebuf.at[w], dbuf.at[w], dkbuf.at[r], dvbuf.at[r],
            )
            for i_, (h, j) in enumerate(tiles):
                obuf[c, h, :, j * DH : (j + 1) * DH] = out[i_ * BLK : (i_ + 1) * BLK]
                dqbuf[c, h, :, j * DH : (j + 1) * DH] = dq[i_ * BLK : (i_ + 1) * BLK]
            for b in range(NB):
                give(obuf, o_hbm, o_s, o_r, c, r * 4 + first + b)
                give(dqbuf, dq_hbm, dq_s, dq_r, c, r * 4 + first + b)
        return carry

    lax.fori_loop(0, CH * 2, work, 0)

    def partial(slot):
        total = None
        for r in range(2):
            for half in range(2):
                rows = slice(half * PLH, (half + 1) * PLH)
                pick = jnp.where(need[r][half] == slot, 1.0, 0.0).astype(F32)
                block = jnp.concatenate(
                    [dkbuf[r, rows] * (pick * SCALE), dvbuf[r, rows] * pick], axis=1
                )
                total = block if total is None else total + block
        return total

    def away(n, carry):
        slot = n * 2 + (1 - core)
        asend[n] = partial(slot).astype(BF)
        send(asend.at[n], arecv.at[n], a_s, a_r.at[n], other_core)
        return carry

    lax.fori_loop(0, 8, away, 0)

    for b in range(8):
        r, at = b // 4, PL + (b % 4) * BLK
        dkvbuf[b, :, :DH] = (dkbuf[r, at : at + BLK] * SCALE).astype(BF)
        dkvbuf[b, :, DH:] = dvbuf[r, at : at + BLK].astype(BF)

        @pl.when(b != me)
        def _():
            send(dkvbuf.at[b], dkv_hbm.at[:, cols(me, WIDE)], dkv_s, dkv_r, (dp, b))

        @pl.when(b == me)
        def _():
            local(dkvbuf.at[b], dkv_hbm.at[:, cols(me, WIDE)], dkv_r)

    for hop, to in ((2, far), (1, up), (3, down)):
        for yy in range(2):
            n = lax.rem(z + hop, 4) * 2 + yy
            drain(arecv.at[n], a_r.at[n])
            bsend[hop - 1, yy] = (partial(n * 2 + core) + arecv[n].astype(F32)).astype(BF)
            send(
                bsend.at[hop - 1, yy], brecv.at[hop - 1, yy], b_s,
                b_r.at[(hop - 1) * 2 + yy], to,
            )

    def gathered(yy):
        n = z * 2 + yy
        total = partial(n * 2 + core) + arecv[n].astype(F32)
        for hop in range(3):
            total += brecv[hop, yy].astype(F32)
        return total

    for yy in range(2):
        drain(arecv.at[z * 2 + yy], a_r.at[z * 2 + yy])
        for hop in range(3):
            drain(brecv.at[hop, yy], b_r.at[hop * 2 + yy])
    csend[...] = gathered(1 - yl).astype(BF)
    send(csend, crecv, c_s, c_r, other_y)
    summed = gathered(yl)
    drain(crecv, c_r)
    gpbuf[...] = (summed + crecv[...].astype(F32)).astype(BF)
    local(gpbuf, gp_hbm, g_s)

    drain(gp_hbm, g_s)
    drain(o_hbm, o_r)
    drain(dq_hbm, dq_r)
    drain(dkv_hbm, dkv_r)
    drain(q_hbm.at[:, : 7 * SPAN], q_s)
    drain(do_hbm.at[:, : 7 * SPAN], do_s)
    drain(kv_hbm.at[:, : 7 * WIDE], kv_s)
    drain(pbuf.at[0:15], p_s)
    drain(obuf.at[:, 0:7], o_s)
    drain(dqbuf.at[:, 0:7], dq_s)
    drain(dkvbuf.at[0:7], dkv_s)
    drain(asend, a_s)
    drain(bsend, b_s)
    drain(csend, c_s)


def body(resp_query, resp_keyval, grad_out, prompt_keyval, response_prompt, piece_owner):
    tok = resp_query.shape[0]
    hbm = pl.BlockSpec(memory_space=pl.ANY)
    smem = pl.BlockSpec(memory_space=pltpu.SMEM)
    dma = pltpu.SemaphoreType.DMA
    shapes = [
        pltpu.VMEM((CH, 8, BLK, CW), BF),
        pltpu.VMEM((CH, 8, BLK, CW), BF),
        pltpu.VMEM((8, BLK, WIDE), BF),
        pltpu.VMEM((16, PLH, WIDE), BF),
        pltpu.VMEM((2, KEYS, DH), BF),
        pltpu.VMEM((2, KEYS, DH), BF),
        pltpu.VMEM((2, DH, KEYS), BF),
        pltpu.VMEM((2, DH + 16, KEYS), BF),
        pltpu.VMEM((2, KEYS, ROWS), F32),
        pltpu.VMEM((2, KEYS, ROWS), BF),
        pltpu.VMEM((2, KEYS, ROWS), BF),
        pltpu.VMEM((2, KEYS, DH), F32),
        pltpu.VMEM((2, KEYS, DH), F32),
        pltpu.VMEM((CH, 8, BLK, CW), BF),
        pltpu.VMEM((CH, 8, BLK, CW), BF),
        pltpu.VMEM((8, BLK, WIDE), BF),
        pltpu.VMEM((8, PLH, WIDE), BF),
        pltpu.VMEM((8, PLH, WIDE), BF),
        pltpu.VMEM((3, 2, PLH, WIDE), BF),
        pltpu.VMEM((3, 2, PLH, WIDE), BF),
        pltpu.VMEM((PLH, WIDE), BF),
        pltpu.VMEM((PLH, WIDE), BF),
        pltpu.VMEM((PLH, WIDE), BF),
    ]
    sems = [
        dma, dma((CH,)), dma, dma((CH,)), dma, dma, dma, dma((16,)),
        dma, dma, dma, dma, dma, dma,
        dma, dma((8,)), dma, dma((6,)), dma, dma, dma,
    ]
    return pl.pallas_call(
        kernel,
        out_shape=[
            jax.ShapeDtypeStruct((tok, 8 * SPAN), BF),
            jax.ShapeDtypeStruct((tok, 8 * SPAN), BF),
            jax.ShapeDtypeStruct((tok, 8 * WIDE), BF),
            jax.ShapeDtypeStruct((PLH, WIDE), BF),
        ],
        in_specs=[hbm, hbm, hbm, hbm, smem, smem],
        out_specs=[hbm, hbm, hbm, hbm],
        scratch_shapes=shapes + sems,
        compiler_params=pltpu.CompilerParams(
            collective_id=0, has_side_effects=True, vmem_limit_bytes=60 * 2**20
        ),
        name="attention",
    )(resp_query, grad_out, resp_keyval, prompt_keyval, response_prompt, piece_owner)


def solution(mesh):
    rows = P(("dp", "head"), None)
    placed = (rows, rows, rows, P("dp", "head"), P("dp"), P())
    return jax.shard_map(
        body,
        mesh=mesh,
        in_specs=placed,
        out_specs=(rows, rows, rows, P("dp", "head")),
        check_vma=False,
    )
```

time: 488 us -> 145 us (0.30); the launches traced: 481 us -> 145 us
  matrix products: 153 us -> 0 us
  local copies, waits for them, and re-layouts: 149 us -> 6.12 us
  Pallas kernels: 0 us -> 138 us
  other arithmetic: 66.9 us -> 0 us
  waiting for transfers between devices: 53.2 us -> 0 us
  starting transfers between devices: 34.1 us -> 0 us
  between operations: 25.1 us -> 0.65 us
    dot_general x18 -> x0, matrix products: 153 us -> none  [the longest x3 31.1 us: back_block(): jnp.einsum('rtkgd,rskd->rkgts', cotangent, value_rows, preferred_element_...]
    pallas_call x0 -> x1, Pallas kernels: none -> 138 us  [body(): pl.pallas_call(kernel, out_shape=[jax.ShapeDtypeStruct((tok, 8 * SPAN), B...]
    all_to_all x6 -> x0, waiting for transfers between devices: 52.5 us -> none  [the longest x1 28.5 us: body(): lax.all_to_all(query3, 'head', split_axis=1, concat_axis=0, tiled=True)]
    unnamed x61 -> x10, local copies, waits for them, and re-layouts: 56.7 us -> 6.12 us
    reshape x8 -> x0, local copies, waits for them, and re-layouts: 37.3 us -> none  [the longest x2 13 us: body(): output_bf.transpose(0, 3, 1, 2, 4)]
    all_to_all x6 -> x0, starting transfers between devices: 34 us -> none  [the longest x1 7.48 us: body(): lax.all_to_all(pair3, 'head', split_axis=1, concat_axis=0, tiled=True)]
    reshape x2 -> x0, other arithmetic: 26.9 us -> none  [the longest x1 14.1 us: body(): output_bf.transpose(0, 3, 1, 2, 4)]
    reduce_sum x3 -> x0, other arithmetic: 21.9 us -> none  [the longest x2 21.7 us: online_update(): normalizer = jnp.sum(weights, axis=-1)]
  transfers between devices with their start and end apart: 8 -> 0, of which waited for: 4 -> 0; matrix products, arithmetic and copies ran while one was open for 45% -> 0% of each run, Pallas kernels for 0% -> 0%
where the time goes in v1:
time: 145 us
  Pallas kernels  138 us (95%)
  local copies, waits for them, and re-layouts  6.12 us (4%)
    pallas_call x1, Pallas kernels, body(): pl.pallas_call(kernel, out_shape=[jax.ShapeDtypeStruct((tok, 8 * SPAN), B...  138 us
    unnamed x10, local copies, waits for them, and re-layouts  6.12 us

profile of v1, /device:TPU:1, one launch (start us, length us, event | category | flops | bytes accessed | tf_op | source)
XLA Modules:
  0.0 144.8 jit_solution(8749333063487921732)
XLA Ops:
  0.6 138.0 %attention.1 = (bf16[128,8192]{1,0:T(8,128)(2,1)}, bf16[128,8192]{1,0:T(8,128)(2,1)}, bf16[128,2048]{1,0:T(8,128)(2,1)}, bf16[512,256]{1,0:T(8,128)(2,1)}) custom-call(bf16[128,8192]{1,0:T(8,128)(2,1)} %q_hbm.1, bf16[128,8192]{1,0:T(8,128)(2,1)} %do_hbm.1, bf16[128,2048]{1,0:T(8,128)(2,1)} %kv_hbm.1, bf16[512,256]{1,0:T(8,128)(2,1)} %pk_hbm.1, s32[2]{0:T(128)} %rp.1, ...), custom_call_target="tpu_custom_call" | custom-call | tf_op jit(solution)/shard_map/attention/pallas_call | solution.py:328
  138.7 0.0 copy-start
  138.7 3.2 %copy.14 = bf16[128,8192]{1,0:T(8,128)(2,1)} copy(bf16[128,8192]{1,0:T(8,128)(2,1)} %get-tuple-element.8) | data formatting | bytes 4194304
  141.9 0.0 copy-done
  141.9 0.0 copy-start.1
  141.9 0.0 copy-start.2
  141.9 1.3 copy.15
  143.3 0.1 copy-done.1
  143.3 0.8 copy.16
  144.1 0.0 copy-done.2
  144.1 0.7 copy.17
Async XLA Ops:
  138.7 3.3 %copy-start = (bf16[128,8192]{1,0:T(8,128)(2,1)S(1)}, bf16[128,8192]{1,0:T(8,128)(2,1)}, u32[]{:S(2)}) copy-start(bf16[128,8192]{1,0:T(8,128)(2,1)} %get-tuple-element.9) | copy-start | bytes 6291460
  141.9 1.4 copy-start.1
  141.9 2.2 %copy-start.2 = (bf16[512,256]{1,0:T(8,128)(2,1)S(1)}, bf16[512,256]{1,0:T(8,128)(2,1)}, u32[]{:S(2)}) copy-start(bf16[512,256]{1,0:T(8,128)(2,1)} %get-tuple-element.11) | copy-start | bytes 786436

commit v2 on v1

--- a/solution.py
+++ b/solution.py
@@ -18,6 +18,9 @@
 SPAN = GROUPS * DH
 
 CH = 4
+HELD = 2
+SPLIT = 4
+PARTS = (4, 4, 1, 1)
 GH = GROUPS // CH
 CW = GH * DH
 NB = 2
@@ -92,12 +95,11 @@
     other_y = (slot_of(z, 1 - yl, core), me)
     up = (slot_of(z + 1, yl, core), me)
     down = (slot_of(z - 1, yl, core), me)
-    far = (slot_of(z + 2, yl, core), me)
     steps = [(1, 1), (3, 1), (2, 0), (2, 1), (0, 1), (1, 0), (3, 0)]
     peers = [lax.rem(x + a, 4) * 2 + lax.rem(yh + b, 2) for a, b in steps]
 
     barrier = pltpu.get_barrier_semaphore()
-    friends = [(dp, h) for h in peers] + [other_core, other_y, up, down, far]
+    friends = [(dp, h) for h in peers] + [other_core, other_y, up, down]
     for friend in friends:
         pl.semaphore_signal(barrier, inc=1, device_id=friend, device_id_type=MESH)
     pl.semaphore_wait(barrier, len(friends))
@@ -113,49 +115,105 @@
     def drain(ref, sem):
         pltpu.make_async_copy(ref, ref, sem).wait()
 
+    def mix(*queues):
+        for turn in range(max(len(queue) for queue in queues)):
+            for queue in queues:
+                if turn < len(queue):
+                    queue[turn]()
+
+    def pieces(src, dst, ssem, rsem, to):
+        rows = src.shape[0] // SPLIT
+        return [
+            functools.partial(
+                send, src.at[pl.ds(n * rows, rows)], dst.at[pl.ds(n * rows, rows)], ssem, rsem, to
+            )
+            for n in range(SPLIT)
+        ]
+
     mine = slot_of(z, yl, core)
-    for to in (other_y, up, down, other_core):
-        send(pk_hbm, pbuf.at[mine], p_s, p_r.at[mine], to)
+    own_half = [
+        pieces(pk_hbm, pbuf.at[mine], p_s, p_r.at[mine], to) for to in (other_y, up, down)
+    ]
+    send(pk_hbm, pbuf.at[mine], p_s, p_r.at[mine], other_core)
     local(pk_hbm, pbuf.at[mine], p_r.at[mine])
 
     def cols(h, width, offset=0):
         return pl.ds(pl.multiple_of(h * (width) + offset, DH), width)
 
-    for h in peers:
-        send(kv_hbm.at[:, cols(h, WIDE)], kvbuf.at[me], kv_s, kv_r, (dp, h))
+    mix(
+        *own_half,
+        [
+            functools.partial(
+                send, kv_hbm.at[:, cols(h, WIDE)], kvbuf.at[me], kv_s, kv_r, (dp, h)
+            )
+            for h in peers
+        ],
+    )
     local(kv_hbm.at[:, cols(me, WIDE)], kvbuf.at[me], kv_r)
 
     def heads_of(h, c):
         return pl.ds(pl.multiple_of(h * SPAN + c * CW, DH), CW)
 
+    def push_one(src, buf, ssem, rsem, c):
+        local(src.at[:, heads_of(me, c)], buf.at[c, me], rsem.at[c])
+        return [
+            functools.partial(
+                send, src.at[:, heads_of(h, c)], buf.at[c, me], ssem, rsem.at[c], (dp, h)
+            )
+            for h in peers
+        ]
+
+    def push_q(c):
+        return push_one(q_hbm, qbuf, q_s, q_r, c)
+
+    def push_do(c):
+        return push_one(do_hbm, dobuf, do_s, do_r, c)
+
     def push(c, carry):
-        for h in peers:
-            send(q_hbm.at[:, heads_of(h, c)], qbuf.at[c, me], q_s, q_r.at[c], (dp, h))
-            send(do_hbm.at[:, heads_of(h, c)], dobuf.at[c, me], do_s, do_r.at[c], (dp, h))
-        local(q_hbm.at[:, heads_of(me, c)], qbuf.at[c, me], q_r.at[c])
-        local(do_hbm.at[:, heads_of(me, c)], dobuf.at[c, me], do_r.at[c])
+        mix(push_q(c), push_do(c))
         return carry
 
-    lax.fori_loop(0, CH, push, 0)
-
-    def forward(slot, targets):
+    def arrived(slot):
         drain(pbuf.at[slot], p_r.at[slot])
-        for to in targets:
-            send(pbuf.at[slot], pbuf.at[slot], p_s, p_r.at[slot], to)
-
-    forward(slot_of(z, 1 - yl, core), (up, down, other_core))
-    forward(slot_of(z + 1, 0, core), (down, other_core))
-    forward(slot_of(z - 1, 1, core), (up, other_core))
-    forward(slot_of(z + 1, 1, core), (other_core,))
-    forward(slot_of(z - 1, 0, core), (other_core,))
-    forward(slot_of(z + 2, 0, core), (other_core,))
-    forward(slot_of(z + 2, 1, core), (other_core,))
+        send(pbuf.at[slot], pbuf.at[slot], p_s, p_r.at[slot], other_core)
+
+    def onward(slot, to):
+        return pieces(pbuf.at[slot], pbuf.at[slot], p_s, p_r.at[slot], to)
+
+    near = slot_of(z, 1 - yl, core)
+    arrived(near)
+    mix(push_q(0), onward(near, up), onward(near, down))
+    arrived(slot_of(z + 1, 0, core))
+    arrived(slot_of(z - 1, 1, core))
+    mix(
+        push_do(0),
+        onward(slot_of(z + 1, 0, core), down),
+        onward(slot_of(z - 1, 1, core), up),
+    )
+    arrived(slot_of(z + 1, 1, core))
+    arrived(slot_of(z - 1, 0, core))
+    mix(push_q(1))
+    dkbuf[...] = jnp.zeros_like(dkbuf)
+    dvbuf[...] = jnp.zeros_like(dvbuf)
+    drain(kvbuf, kv_r)
+    for r in range(2):
+        for b in range(4):
+            rows = slice(PL + b * BLK, PL + (b + 1) * BLK)
+            both = kvbuf[r * 4 + b]
+            kbuf[r, rows] = both[:, :DH]
+            vbuf[r, rows] = both[:, DH:]
+            ktbuf[r, :, rows] = both[:, :DH].T
+            vtbuf[r, :DH, rows] = both[:, DH:].T
+        vtbuf[r, DH:] = jnp.ones((16, KEYS), BF)
+    arrived(slot_of(z + 2, 0, core))
+    arrived(slot_of(z + 2, 1, core))
+    mix(push_do(1))
+    lax.fori_loop(2, CH, push, 0)
     drain(pbuf.at[mine], p_r.at[mine])
     for zz in range(4):
         for yy in range(2):
             slot = slot_of(zz, yy, 1 - core)
             drain(pbuf.at[slot], p_r.at[slot])
-    drain(kvbuf, kv_r)
 
     need = [[po[2 * rp[r] + half] for half in range(2)] for r in range(2)]
     for r in range(2):
@@ -166,25 +224,20 @@
             vbuf[r, rows] = both[:, DH:]
             ktbuf[r, :, rows] = both[:, :DH].T
             vtbuf[r, :DH, rows] = both[:, DH:].T
-        for b in range(4):
-            rows = slice(PL + b * BLK, PL + (b + 1) * BLK)
-            both = kvbuf[r * 4 + b]
-            kbuf[r, rows] = both[:, :DH]
-            vbuf[r, rows] = both[:, DH:]
-            ktbuf[r, :, rows] = both[:, :DH].T
-            vtbuf[r, :DH, rows] = both[:, DH:].T
-        vtbuf[r, DH:] = jnp.ones((16, KEYS), BF)
-    dkbuf[...] = jnp.zeros_like(dkbuf)
-    dvbuf[...] = jnp.zeros_like(dvbuf)
-
-    def give(buf, hbm, ssem, rsem, c, h):
-        @pl.when(h != me)
-        def _():
-            send(buf.at[c, h], hbm.at[:, heads_of(me, c)], ssem, rsem, (dp, h))
-
-        @pl.when(h == me)
-        def _():
-            local(buf.at[c, h], hbm.at[:, heads_of(me, c)], rsem)
+
+    def give(c):
+        queues = []
+        for buf, hbm, ssem, rsem in ((obuf, o_hbm, o_s, o_r), (dqbuf, dq_hbm, dq_s, dq_r)):
+            local(buf.at[c, me], hbm.at[:, heads_of(me, c)], rsem)
+            queues.append(
+                [
+                    functools.partial(
+                        send, buf.at[c, h], hbm.at[:, heads_of(me, c)], ssem, rsem, (dp, h)
+                    )
+                    for h in peers
+                ]
+            )
+        return queues
 
     def work(i, carry):
         c, r = i // 2, lax.rem(i, 2)
@@ -206,9 +259,11 @@
             for i_, (h, j) in enumerate(tiles):
                 obuf[c, h, :, j * DH : (j + 1) * DH] = out[i_ * BLK : (i_ + 1) * BLK]
                 dqbuf[c, h, :, j * DH : (j + 1) * DH] = dq[i_ * BLK : (i_ + 1) * BLK]
-            for b in range(NB):
-                give(obuf, o_hbm, o_s, o_r, c, r * 4 + first + b)
-                give(dqbuf, dq_hbm, dq_s, dq_r, c, r * 4 + first + b)
+
+        @pl.when((r == 1) & (c < CH - HELD))
+        def _():
+            mix(*give(c))
+
         return carry
 
     lax.fori_loop(0, CH * 2, work, 0)
@@ -225,53 +280,62 @@
                 total = block if total is None else total + block
         return total
 
-    def away(n, carry):
-        slot = n * 2 + (1 - core)
-        asend[n] = partial(slot).astype(BF)
+    def pair_of(hop, yy):
+        return lax.rem(z + hop, 4) * 2 + yy
+
+    order = [(2, 0), (2, 1), (1, 1), (3, 0), (1, 0), (3, 1), (0, 0), (0, 1)]
+    for hop, yy in order:
+        n = pair_of(hop, yy)
+        asend[n] = partial(n * 2 + (1 - core)).astype(BF)
         send(asend.at[n], arecv.at[n], a_s, a_r.at[n], other_core)
-        return carry
-
-    lax.fori_loop(0, 8, away, 0)
+
+    def own_pair(hop, yy):
+        n = pair_of(hop, yy)
+        total = partial(n * 2 + core)
+        drain(arecv.at[n], a_r.at[n])
+        return total + arecv[n].astype(F32)
+
+    def along(i, value, to):
+        bsend[i] = value.astype(BF)
+        return pieces(bsend.at[i], brecv.at[i], b_s, b_r.at[i], to)
+
+    first_up = along(0, own_pair(2, 0), up)
+    first_down = along(1, own_pair(2, 1), down)
+    mix(first_up, first_down)
+    second_up = along(2, own_pair(1, 1), up)
+    second_down = along(3, own_pair(3, 0), down)
+    mix(second_up, second_down, *give(CH - 2))
+    last = []
+    for i, hop, yy, to in ((0, 1, 0, up), (1, 3, 1, down)):
+        total = own_pair(hop, yy)
+        drain(brecv.at[i], b_r.at[i])
+        last.append(along(4 + i, total + brecv[i].astype(F32), to))
 
     for b in range(8):
         r, at = b // 4, PL + (b % 4) * BLK
         dkvbuf[b, :, :DH] = (dkbuf[r, at : at + BLK] * SCALE).astype(BF)
         dkvbuf[b, :, DH:] = dvbuf[r, at : at + BLK].astype(BF)
-
-        @pl.when(b != me)
-        def _():
-            send(dkvbuf.at[b], dkv_hbm.at[:, cols(me, WIDE)], dkv_s, dkv_r, (dp, b))
-
-        @pl.when(b == me)
-        def _():
-            local(dkvbuf.at[b], dkv_hbm.at[:, cols(me, WIDE)], dkv_r)
-
-    for hop, to in ((2, far), (1, up), (3, down)):
-        for yy in range(2):
-            n = lax.rem(z + hop, 4) * 2 + yy
-            drain(arecv.at[n], a_r.at[n])
-            bsend[hop - 1, yy] = (partial(n * 2 + core) + arecv[n].astype(F32)).astype(BF)
-            send(
-                bsend.at[hop - 1, yy], brecv.at[hop - 1, yy], b_s,
-                b_r.at[(hop - 1) * 2 + yy], to,
-            )
-
-    def gathered(yy):
-        n = z * 2 + yy
-        total = partial(n * 2 + core) + arecv[n].astype(F32)
-        for hop in range(3):
-            total += brecv[hop, yy].astype(F32)
-        return total
-
-    for yy in range(2):
-        drain(arecv.at[z * 2 + yy], a_r.at[z * 2 + yy])
-        for hop in range(3):
-            drain(brecv.at[hop, yy], b_r.at[hop * 2 + yy])
-    csend[...] = gathered(1 - yl).astype(BF)
-    send(csend, crecv, c_s, c_r, other_y)
-    summed = gathered(yl)
+    pairs_out = [
+        functools.partial(
+            send, dkvbuf.at[h], dkv_hbm.at[:, cols(me, WIDE)], dkv_s, dkv_r, (dp, h)
+        )
+        for h in peers
+    ]
+    local(dkvbuf.at[me], dkv_hbm.at[:, cols(me, WIDE)], dkv_r)
+    mix(*last, pairs_out, *give(CH - 1))
+
+    zero_half = own_pair(0, 0)
+    one_half = own_pair(0, 1)
+    for i in (2, 3, 4, 5):
+        drain(brecv.at[i], b_r.at[i])
+    zero_half += brecv[3].astype(F32) + brecv[4].astype(F32)
+    one_half += brecv[2].astype(F32) + brecv[5].astype(F32)
+    low = yl == 0
+    csend[...] = jnp.where(low, one_half, zero_half).astype(BF)
+    mix(pieces(csend, crecv, c_s, c_r, other_y))
+    kept = jnp.where(low, zero_half, one_half)
     drain(crecv, c_r)
-    gpbuf[...] = (summed + crecv[...].astype(F32)).astype(BF)
+    gpbuf[...] = (kept + crecv[...].astype(F32)).astype(BF)
     local(gpbuf, gp_hbm, g_s)
 
     drain(gp_hbm, g_s)
@@ -288,6 +352,29 @@
     drain(asend, a_s)
     drain(bsend, b_s)
     drain(csend, c_s)
+
+
+def settle(*refs):
+    sources, targets, stages = refs[:4], refs[4:8], refs[8:12]
+    into, out = refs[12:]
+    moves = []
+    for src, dst, stage, parts in zip(sources, targets, stages, PARTS):
+        rows = src.shape[0] // parts
+        for n in range(parts):
+            at, i = pl.ds(n * rows, rows), len(moves)
+            moves.append(
+                (
+                    pltpu.make_async_copy(src.at[at], stage.at[at], into.at[i]),
+                    pltpu.make_async_copy(stage.at[at], dst.at[at], out.at[i]),
+                )
+            )
+    for first, _ in moves:
+        first.start()
+    for first, second in moves:
+        first.wait()
+        second.start()
+    for _, second in moves:
+        second.wait()
 
 
 def body(resp_query, resp_keyval, grad_out, prompt_keyval, response_prompt, piece_owner):
@@ -314,8 +401,8 @@
         pltpu.VMEM((8, BLK, WIDE), BF),
         pltpu.VMEM((8, PLH, WIDE), BF),
         pltpu.VMEM((8, PLH, WIDE), BF),
-        pltpu.VMEM((3, 2, PLH, WIDE), BF),
-        pltpu.VMEM((3, 2, PLH, WIDE), BF),
+        pltpu.VMEM((6, PLH, WIDE), BF),
+        pltpu.VMEM((6, PLH, WIDE), BF),
         pltpu.VMEM((PLH, WIDE), BF),
         pltpu.VMEM((PLH, WIDE), BF),
         pltpu.VMEM((PLH, WIDE), BF),
@@ -325,7 +412,7 @@
         dma, dma, dma, dma, dma, dma,
         dma, dma((8,)), dma, dma((6,)), dma, dma, dma,
     ]
-    return pl.pallas_call(
+    made = pl.pallas_call(
         kernel,
         out_shape=[
             jax.ShapeDtypeStruct((tok, 8 * SPAN), BF),
@@ -341,6 +428,15 @@
         ),
         name="attention",
     )(resp_query, grad_out, resp_keyval, prompt_keyval, response_prompt, piece_owner)
+    return pl.pallas_call(
+        settle,
+        out_shape=[jax.ShapeDtypeStruct(a.shape, a.dtype) for a in made],
+        in_specs=[hbm] * 4,
+        out_specs=[hbm] * 4,
+        scratch_shapes=[pltpu.VMEM(a.shape, a.dtype) for a in made] + [dma((sum(PARTS),))] * 2,
+        compiler_params=pltpu.CompilerParams(vmem_limit_bytes=60 * 2**20),
+        name="settle",
+    )(*made)
 
 
 def solution(mesh):

time: 145 us -> 131 us (0.903)
  Pallas kernels: 138 us -> 130 us
  local copies, waits for them, and re-layouts: 6.12 us -> 0 us
    pallas_call x1, Pallas kernels: 138 us -> 125 us  [body(): pl.pallas_call(kernel, out_shape=[jax.ShapeDtypeStruct((tok, 8 * SPAN), B...]
    unnamed x10 -> x0, local copies, waits for them, and re-layouts: 6.12 us -> none
    pallas_call x0 -> x1, Pallas kernels: none -> 4.34 us  [body(): pl.pallas_call(settle, out_shape=[jax.ShapeDtypeStruct(a.shape, a.dtype)...]
where the time goes in v2:
time: 131 us; the launch traced here: 130 us
  Pallas kernels  130 us (99%)
    pallas_call x1, Pallas kernels, body(): pl.pallas_call(kernel, out_shape=[jax.ShapeDtypeStruct((tok, 8 * SPAN), B...  125 us
    pallas_call x1, Pallas kernels, body(): pl.pallas_call(settle, out_shape=[jax.ShapeDtypeStruct(a.shape, a.dtype)...  4.34 us

profile of v2, /device:TPU:1, one launch (start us, length us, event | category | flops | bytes accessed | tf_op | source)
XLA Modules:
  0.0 130.2 jit_solution(15986618709737226742)
XLA Ops:
  0.6 125.2 %attention.1 = (bf16[128,8192]{1,0:T(8,128)(2,1)}, bf16[128,8192]{1,0:T(8,128)(2,1)}, bf16[128,2048]{1,0:T(8,128)(2,1)}, bf16[512,256]{1,0:T(8,128)(2,1)}) custom-call(bf16[128,8192]{1,0:T(8,128)(2,1)} %q_hbm.1, bf16[128,8192]{1,0:T(8,128)(2,1)} %do_hbm.1, bf16[128,2048]{1,0:T(8,128)(2,1)} %kv_hbm.1, bf16[512,256]{1,0:T(8,128)(2,1)} %pk_hbm.1, s32[2]{0:T(128)} %rp.1, ...), custom_call_target="tpu_custom_call" | custom-call | tf_op jit(solution)/shard_map/attention/pallas_call | solution.py:415
  125.9 4.3 %settle.1 = (bf16[128,8192]{1,0:T(8,128)(2,1)}, bf16[128,8192]{1,0:T(8,128)(2,1)}, bf16[128,2048]{1,0:T(8,128)(2,1)}, bf16[512,256]{1,0:T(8,128)(2,1)}) custom-call(bf16[128,8192]{1,0:T(8,128)(2,1)} %get-tuple-element.8.refs_0_, bf16[128,8192]{1,0:T(8,128)(2,1)} %get-tuple-element.9.refs_1_, bf16[128,2048]{1,0:T(8,128)(2,1)} %get-tuple-element.10.refs_2_, ...), custom_call_target="tpu_custom_call" | custom-call | tf_op jit(solution)/shard_map/settle/pallas_call | solution.py:431

commit v3 on v2

--- a/solution.py
+++ b/solution.py
@@ -19,8 +19,8 @@
 
 CH = 4
 HELD = 2
-SPLIT = 4
-PARTS = (4, 4, 1, 1)
+SPLIT = 2
+PARTS = (1, 1, 1, 1)
 GH = GROUPS // CH
 CW = GH * DH
 NB = 2
@@ -95,7 +95,7 @@
     other_y = (slot_of(z, 1 - yl, core), me)
     up = (slot_of(z + 1, yl, core), me)
     down = (slot_of(z - 1, yl, core), me)
-    steps = [(1, 1), (3, 1), (2, 0), (2, 1), (0, 1), (1, 0), (3, 0)]
+    steps = [(2, 1), (1, 0), (3, 1), (2, 0), (1, 1), (3, 0), (0, 1)]
     peers = [lax.rem(x + a, 4) * 2 + lax.rem(yh + b, 2) for a, b in steps]
 
     barrier = pltpu.get_barrier_semaphore()
@@ -182,17 +182,17 @@
 
     near = slot_of(z, 1 - yl, core)
     arrived(near)
-    mix(push_q(0), onward(near, up), onward(near, down))
+    mix(onward(near, up), onward(near, down), push_q(0), push_do(0))
     arrived(slot_of(z + 1, 0, core))
     arrived(slot_of(z - 1, 1, core))
     mix(
-        push_do(0),
+        push_q(1),
         onward(slot_of(z + 1, 0, core), down),
         onward(slot_of(z - 1, 1, core), up),
     )
     arrived(slot_of(z + 1, 1, core))
     arrived(slot_of(z - 1, 0, core))
-    mix(push_q(1))
+    mix(push_do(1))
     dkbuf[...] = jnp.zeros_like(dkbuf)
     dvbuf[...] = jnp.zeros_like(dvbuf)
     drain(kvbuf, kv_r)
@@ -207,7 +207,6 @@
         vtbuf[r, DH:] = jnp.ones((16, KEYS), BF)
     arrived(slot_of(z + 2, 0, core))
     arrived(slot_of(z + 2, 1, core))
-    mix(push_do(1))
     lax.fori_loop(2, CH, push, 0)
     drain(pbuf.at[mine], p_r.at[mine])
     for zz in range(4):

time: 131 us -> 127 us (0.969)
  Pallas kernels: 130 us -> 126 us
    pallas_call x1, Pallas kernels: 125 us -> 123 us  [body(): pl.pallas_call(kernel, out_shape=[jax.ShapeDtypeStruct((tok, 8 * SPAN), B...]
where the time goes in v3:
time: 127 us
  Pallas kernels  126 us (99%)
    pallas_call x1, Pallas kernels, body(): pl.pallas_call(kernel, out_shape=[jax.ShapeDtypeStruct((tok, 8 * SPAN), B...  123 us
    pallas_call x1, Pallas kernels, body(): pl.pallas_call(settle, out_shape=[jax.ShapeDtypeStruct(a.shape, a.dtype)...  3.9 us

profile of v3, /device:TPU:1, one launch (start us, length us, event | category | flops | bytes accessed | tf_op | source)
XLA Modules:
  0.0 127.1 jit_solution(11373735940231929398)
XLA Ops:
  0.6 122.5 %attention.1 = (bf16[128,8192]{1,0:T(8,128)(2,1)}, bf16[128,8192]{1,0:T(8,128)(2,1)}, bf16[128,2048]{1,0:T(8,128)(2,1)}, bf16[512,256]{1,0:T(8,128)(2,1)}) custom-call(bf16[128,8192]{1,0:T(8,128)(2,1)} %q_hbm.1, bf16[128,8192]{1,0:T(8,128)(2,1)} %do_hbm.1, bf16[128,2048]{1,0:T(8,128)(2,1)} %kv_hbm.1, bf16[512,256]{1,0:T(8,128)(2,1)} %pk_hbm.1, s32[2]{0:T(128)} %rp.1, ...), custom_call_target="tpu_custom_call" | custom-call | tf_op jit(solution)/shard_map/attention/pallas_call | solution.py:414
  123.2 3.9 %settle.1 = (bf16[128,8192]{1,0:T(8,128)(2,1)}, bf16[128,8192]{1,0:T(8,128)(2,1)}, bf16[128,2048]{1,0:T(8,128)(2,1)}, bf16[512,256]{1,0:T(8,128)(2,1)}) custom-call(bf16[128,8192]{1,0:T(8,128)(2,1)} %get-tuple-element.8.refs_0_, bf16[128,8192]{1,0:T(8,128)(2,1)} %get-tuple-element.9.refs_1_, bf16[128,2048]{1,0:T(8,128)(2,1)} %get-tuple-element.10.refs_2_, ...), custom_call_target="tpu_custom_call" | custom-call | tf_op jit(solution)/shard_map/settle/pallas_call | solution.py:430

commit v4 on v3

--- a/solution.py
+++ b/solution.py
@@ -18,7 +18,7 @@
 SPAN = GROUPS * DH
 
 CH = 4
-HELD = 2
+HELD = 1
 SPLIT = 2
 PARTS = (1, 1, 1, 1)
 GH = GROUPS // CH
@@ -303,7 +303,7 @@
     mix(first_up, first_down)
     second_up = along(2, own_pair(1, 1), up)
     second_down = along(3, own_pair(3, 0), down)
-    mix(second_up, second_down, *give(CH - 2))
+    mix(second_up, second_down)
     last = []
     for i, hop, yy, to in ((0, 1, 0, up), (1, 3, 1, down)):
         total = own_pair(hop, yy)

time: 127 us -> 127 us (level)
  no operation moved by 1% of the time
where the time goes in v4:
time: 127 us
  Pallas kernels  126 us (99%)
    pallas_call x1, Pallas kernels, body(): pl.pallas_call(kernel, out_shape=[jax.ShapeDtypeStruct((tok, 8 * SPAN), B...  123 us
    pallas_call x1, Pallas kernels, body(): pl.pallas_call(settle, out_shape=[jax.ShapeDtypeStruct(a.shape, a.dtype)...  3.9 us

profile of v4, /device:TPU:1, one launch (start us, length us, event | category | flops | bytes accessed | tf_op | source)
XLA Modules:
  0.0 127.1 jit_solution(2633976155565328525)
XLA Ops:
  0.6 122.5 %attention.1 = (bf16[128,8192]{1,0:T(8,128)(2,1)}, bf16[128,8192]{1,0:T(8,128)(2,1)}, bf16[128,2048]{1,0:T(8,128)(2,1)}, bf16[512,256]{1,0:T(8,128)(2,1)}) custom-call(bf16[128,8192]{1,0:T(8,128)(2,1)} %q_hbm.1, bf16[128,8192]{1,0:T(8,128)(2,1)} %do_hbm.1, bf16[128,2048]{1,0:T(8,128)(2,1)} %kv_hbm.1, bf16[512,256]{1,0:T(8,128)(2,1)} %pk_hbm.1, s32[2]{0:T(128)} %rp.1, ...), custom_call_target="tpu_custom_call" | custom-call | tf_op jit(solution)/shard_map/attention/pallas_call | solution.py:414
  123.2 3.9 %settle.1 = (bf16[128,8192]{1,0:T(8,128)(2,1)}, bf16[128,8192]{1,0:T(8,128)(2,1)}, bf16[128,2048]{1,0:T(8,128)(2,1)}, bf16[512,256]{1,0:T(8,128)(2,1)}) custom-call(bf16[128,8192]{1,0:T(8,128)(2,1)} %get-tuple-element.8.refs_0_, bf16[128,8192]{1,0:T(8,128)(2,1)} %get-tuple-element.9.refs_1_, bf16[128,2048]{1,0:T(8,128)(2,1)} %get-tuple-element.10.refs_2_, ...), custom_call_target="tpu_custom_call" | custom-call | tf_op jit(solution)/shard_map/settle/pallas_call | solution.py:430
